TPU v7x, 32 devices: a whole 2x2x4 slice. The times are simulated.
32 devices in a mesh: rows: 16 (over z, y, core), rank: 2 (over x).
Axes of the slice: x: 2, y: 2, z: 4, core: 2. Of those that a mesh axis runs over, the one named last changes fastest.
Arguments:
- factor: bfloat16 [16384, 16384], P('rows', 'rank'), may hold values from -0.046875 to 0.046875
- probes: bfloat16 [16384, 256], P('rows'), may hold values from -1.5 to 1.5
- cotangent: bfloat16 [16384, 256], P('rows'), may hold values from -1.5 to 1.5
- core_inverse: bfloat16 [16384, 2, 8192], P('rank', None, 'rows'), may hold values from -0.046875 to 0.046875
- pivots: int32 [16384], replicated, may hold values from 0 to 16383, as said below
- noise: float32 [1], replicated, may hold values from 0.5 to 2
Outputs:
- probe_grad: bfloat16 [16384, 256], P('rows')
- factor_grad: bfloat16 [16384, 16384], P('rows', 'rank')
Inputs may be any that keep to these rules, and one draw needn't show every extreme that they name: `pivots`: distinct slab rows; rows 0 and 16383 are always among them.
All inputs are finite; a program needn't handle non-finite values.
Results may differ from a plain program's by a relative error of at most 0.001.
Values sent between devices are 32-bit elements; how exact they have to be, the bound alone decides.
A program may use at most 128 MiB of HBM per device.

v0:
```python
import jax
import jax.numpy as jnp
from jax import lax
from jax.sharding import PartitionSpec as P


def body(factor, probes, cotangent, core_inverse, pivots, noise):
    highest = lax.Precision.HIGHEST
    rows_dev = factor.shape[0]
    block_cols = factor.shape[1]
    width = probes.shape[1]
    n_rows = lax.axis_size("rows")
    n_rank = lax.axis_size("rank")
    slim = block_cols // n_rows
    row_index = lax.axis_index("rows")
    rank_index = lax.axis_index("rank")
    scale = noise[0]
    core_tile = core_inverse.reshape(block_cols, n_rank * slim).astype(jnp.float32)
    contract = (((0,), (0,)), ((), ()))
    stacked = jnp.concatenate([probes, cotangent], axis=1)
    partial_sums = lax.dot_general(factor, stacked, contract, preferred_element_type=jnp.float32)
    share = lax.psum_scatter(partial_sums, "rows", scatter_dimension=0, tiled=True)
    coef_part = share[:, :width]
    dual_full = lax.all_gather(share[:, width:], "rows", axis=0, tiled=True)
    coef_cols = lax.all_gather(coef_part, "rank", axis=0, tiled=True)
    weights_blk = lax.psum(
        jnp.dot(core_tile, coef_cols, precision=highest, preferred_element_type=jnp.float32), "rows"
    )
    dual_part = lax.psum_scatter(
        lax.dot_general(
            core_tile, dual_full, contract, precision=highest, preferred_element_type=jnp.float32
        ),
        "rank",
        scatter_dimension=0,
        tiled=True,
    )
    duals_blk = lax.all_gather(dual_part, "rows", axis=0, tiled=True)
    local_product = jnp.dot(
        factor.astype(jnp.float32), duals_blk, precision=highest, preferred_element_type=jnp.float32
    )
    correction = lax.psum(local_product, "rank")
    probe_grad = ((cotangent.astype(jnp.float32) - correction) / scale).astype(jnp.bfloat16)
    left_side = jnp.concatenate([cotangent, probes], axis=1).astype(jnp.float32)
    right_side = jnp.concatenate([weights_blk, duals_blk], axis=1)
    outer_sum = lax.dot_general(
        left_side,
        right_side,
        (((1,), (1,)), ((), ())),
        precision=highest,
        preferred_element_type=jnp.float32,
    )
    grads = -outer_sum / scale
    local_rows = pivots - row_index * rows_dev
    inside = (local_rows >= 0) & (local_rows < rows_dev)
    target = jnp.where(inside, local_rows, rows_dev)
    total_rank = pivots.shape[0]
    pivot_rank = (
        jnp.full((rows_dev + 1,), total_rank, jnp.int32)
        .at[target]
        .set(jnp.arange(total_rank, dtype=jnp.int32))[:rows_dev]
    )
    columns = rank_index * block_cols + jnp.arange(block_cols, dtype=jnp.int32)
    grads = jnp.where(columns[None, :] > pivot_rank[:, None], jnp.float32(0.0), grads)
    return (probe_grad, grads.astype(jnp.bfloat16))


def solution(mesh):
    placed = (
        P("rows", "rank"),
        P("rows", None),
        P("rows", None),
        P("rank", None, "rows"),
        P(),
        P(),
    )
    return jax.shard_map(
        body,
        mesh=mesh,
        in_specs=placed,
        out_specs=(P("rows", None), P("rows", "rank")),
        check_vma=False,
    )
```

profile of v0, /device:TPU:0, one launch (start us, length us, event | category | flops | bytes accessed | tf_op | source)
XLA Modules:
  0.0 642.8 jit_solution(9772494841048444390)
XLA Ops:
  7.2 0.0 reduce-scatter.3.cloned.1.call-start
  7.2 16.2 %convolution_bitcast_fusion = f32[8192,512]{0,1:T(8,128)} fusion(bf16[1024,8192]{1,0:T(8,128)(2,1)} %param.6, bf16[1024,256]{1,0:T(8,128)(2,1)} %param.8, bf16[1024,256]{1,0:T(8,128)(2,1)} %param.7), kind=kOutput, calls=%fused_computation.5 | convolution fusion | flops 8592031744 | bytes 34603008 | tf_op jit(solution)/shard_map/dot_general | solution.py:21
  23.4 0.0 reduce-scatter.3.cloned.1.call-update
  23.4 0.0 all-gather.4.cloned.1.call-start
  23.5 181.4 %reduce-scatter.3.cloned.1.call-done = f32[512,512]{0,1:T(8,128)} async-done(((f32[8192,512]{0,1:T(8,128)}), f32[512,512]{0,1:T(8,128)}) %reduce-scatter.3.cloned.1.call-update) | async-done | bytes 1048592 | tf_op jit(solution)/shard_map/reduce_scatter | solution.py:22
  204.8 2.3 fusion.14
  207.1 0.0 all-gather.4.cloned.1.call-update
  207.1 0.0 reduce-scatter.5.cloned.1.call-start
  207.2 16.6 %copy.10 = bf16[1024,8,2,512]{3,1,2,0:T(8,128)(2,1)} copy(bf16[1024,8,2,512]{3,2,1,0:T(2,128)(2,1)} %bitcast.20) | data formatting | bytes 33554432
  223.8 57.4 %all-gather.4.cloned.1.call-done = f32[8192,256]{0,1:T(8,128)} async-done(((f32[512,256]{0,1:T(8,128)}), f32[8192,256]{0,1:T(8,128)}) %all-gather.4.cloned.1.call-update) | async-done | bytes 8388624 | tf_op jit(solution)/shard_map/all_gather | solution.py:24
  281.2 18.6 %convolution_bitcast_fusion.3 = f32[1024,256]{0,1:T(8,128)} fusion(f32[8192,256]{0,1:T(8,128)} %all-gather.4.cloned.1.call-done, bf16[8192,1024]{1,0:T(8,128)(2,1)} %bitcast.21), kind=kOutput, calls=%fused_computation.8 | convolution fusion | flops 25769803776 | bytes 26214400 | tf_op jit(solution)/shard_map/dot_general | solution.py:30
  299.8 0.0 reduce-scatter.5.cloned.1.call-update
  299.8 0.0 all-gather.8.cloned.1.call-start
  299.8 0.5 all-gather.8.cloned.1.call-update
  300.4 0.0 all-gather.6.cloned.1.call-start
  300.4 18.1 %reduce-scatter.5.cloned.1.call-done = f32[512,256]{0,1:T(8,128)} async-done(((f32[1024,256]{0,1:T(8,128)}), f32[512,256]{0,1:T(8,128)}) %reduce-scatter.5.cloned.1.call-update) | async-done | bytes 524304 | tf_op jit(solution)/shard_map/reduce_scatter | solution.py:29
  318.5 0.0 all-gather.6.cloned.1.call-update
  318.6 0.2 all-reduce.5.cloned.1.call-start
  318.8 23.1 %all-gather.8.cloned.1.call-done = f32[1024,256]{0,1:T(8,128)} async-done(((f32[512,256]{0,1:T(8,128)}), f32[1024,256]{0,1:T(8,128)}) %all-gather.8.cloned.1.call-update) | async-done | bytes 1048592 | tf_op jit(solution)/shard_map/all_gather | solution.py:25
  341.9 18.6 %convolution_bitcast_fusion.1 = f32[8192,256]{0,1:T(8,128)} fusion(f32[1024,256]{0,1:T(8,128)} %all-gather.8.cloned.1.call-done, bf16[8192,1024]{1,0:T(8,128)(2,1)} %bitcast.22), kind=kOutput, calls=%fused_computation.6 | convolution fusion | flops 25769803776 | bytes 26214400 | tf_op jit(solution)/shard_map/dot_general | solution.py:27
  360.5 0.0 all-reduce.5.cloned.1.call-update
  360.5 0.0 all-reduce.3.cloned.1.call-start
  360.6 0.2 copy.8
  360.8 60.3 %scatter_custom_fusion = s32[1025]{0:T(1024)S(1)} fusion(s32[16384]{0:T(1024)S(1)} %compare_select_fusion, s32[16384]{0:T(1024)S(1)} %iota.9, s32[]{:T(128)} %constant.3.clone.1), kind=kCustom, calls=%fused_computation.18 | custom fusion | bytes 4104 | tf_op jit(solution)/shard_map/scatter | solution.py:60
  421.9 0.0 all-gather.6.cloned.1.call-done
  421.9 18.5 %convolution_bitcast_fusion.2 = f32[1024,256]{0,1:T(8,128)} fusion(f32[8192,256]{0,1:T(8,128)} %all-gather.6.cloned.1.call-done, bf16[1024,8192]{1,0:T(8,128)(2,1)} %param.6), kind=kOutput, calls=%fused_computation.7 | convolution fusion | flops 25769803776 | bytes 26214400 | tf_op jit(solution)/shard_map/dot_general | solution.py:38
  440.4 0.0 all-reduce.3.cloned.1.call-update
  440.4 150.9 %all-reduce.5.cloned.1.call-done = f32[8192,256]{0,1:T(8,128)} async-done(((f32[8192,256]{0,1:T(8,128)}), f32[8192,256]{0,1:T(8,128)}) %all-reduce.5.cloned.1.call-update) | async-done | bytes 8388624 | tf_op jit(solution)/shard_map/psum | solution.py:26
  591.4 33.5 %select_convert_fusion = bf16[1024,8192]{1,0:T(8,128)(2,1)} fusion(f32[8192,256]{0,1:T(8,128)} %all-gather.6.cloned.1.call-done, f32[8192,256]{0,1:T(8,128)} %all-reduce.5.cloned.1.call-done, f32[]{:T(128)} %bitcast.19, s32[8192]{0:T(1024)S(1)} %iota_add_fusion, s32[1024]{0:T(1024)S(1)} %slice.13, bf16[1024,256]{1,0:T(8,128)(2,1)S(1)} %copy-done.1, ...), kind=kOutput, calls=%fused_computation.1 | convolution fusion | flops 51587842048 | bytes 34639876 | tf_op jit(solution)/shard_map/dot_general | solution.py:45
  624.8 8.7 %all-reduce.3.cloned.1.call-done = f32[1024,256]{0,1:T(8,128)} async-done(((f32[1024,256]{0,1:T(8,128)}), f32[1024,256]{0,1:T(8,128)}) %all-reduce.3.cloned.1.call-update) | async-done | bytes 1048592 | tf_op jit(solution)/shard_map/psum | solution.py:41
  633.6 1.4 divide_convert_fusion
  635.0 1.0 copy.9
  (10 shorter events, 0.1 us)
Async XLA Ops:
  7.2 197.7 %reduce-scatter.3.cloned.1.call-start = ((), (), s32[]{:S(2)}) async-start(), calls=%async_computation.2 | async-start | bytes 17825792 | tf_op jit(solution)/shard_map/reduce_scatter | solution.py:22
  23.4 257.8 %all-gather.4.cloned.1.call-start = ((), (), s32[]{:S(2)}) async-start(), calls=%async_computation.3 | async-start | bytes 8912896 | tf_op jit(solution)/shard_map/all_gather | solution.py:24
  207.1 111.4 %reduce-scatter.5.cloned.1.call-start = ((), (), s32[]{:S(2)}) async-start(), calls=%async_computation.4 | async-start | bytes 1572864 | tf_op jit(solution)/shard_map/reduce_scatter | solution.py:29
  299.8 42.1 %all-gather.8.cloned.1.call-start = ((), (), s32[]{:S(2)}) async-start(), calls=%async_computation.7 | async-start | bytes 1572864 | tf_op jit(solution)/shard_map/all_gather | solution.py:25
  300.4 121.5 %all-gather.6.cloned.1.call-start = ((), (), s32[]{:S(2)}) async-start(), calls=%async_computation.5 | async-start | bytes 8912896 | tf_op jit(solution)/shard_map/all_gather | solution.py:37
  318.5 42.0 %copy-start = (bf16[1024,256]{1,0:T(8,128)(2,1)S(1)}, bf16[1024,256]{1,0:T(8,128)(2,1)}, u32[]{:S(2)}) copy-start(bf16[1024,256]{1,0:T(8,128)(2,1)} %param.8) | copy-start | bytes 1572868
  318.5 42.3 %copy-start.2 = (s32[16384]{0:T(1024)S(1)}, s32[16384]{0:T(1024)}, u32[]{:S(2)}) copy-start(s32[16384]{0:T(1024)} %param.10) | copy-start | bytes 196612
  318.6 272.8 %all-reduce.5.cloned.1.call-start = ((), (), s32[]{:S(2)}) async-start(), calls=%async_computation.8 | async-start | bytes 16777216 | tf_op jit(solution)/shard_map/psum | solution.py:26
  360.5 273.1 %all-reduce.3.cloned.1.call-start = ((), (), s32[]{:S(2)}) async-start(), calls=%async_computation.6 | async-start | bytes 2097152 | tf_op jit(solution)/shard_map/psum | solution.py:41
  421.8 169.5 %copy-start.1 = (bf16[1024,256]{1,0:T(8,128)(2,1)S(1)}, bf16[1024,256]{1,0:T(8,128)(2,1)}, u32[]{:S(2)}) copy-start(bf16[1024,256]{1,0:T(8,128)(2,1)} %param.7) | copy-start | bytes 1572868
Sparse Core Ops, SparseCore 0:
  23.5 181.2 reduce-scatter.2
  207.2 73.9 all-gather.3
  299.9 18.5 reduce-scatter.4
  320.6 21.2 all-gather.7
  344.2 74.9 all-gather.5
  423.2 168.1 all-reduce.4
  593.6 39.8 all-reduce.2
where the time goes:
time: 643 us
  waiting for transfers between devices  440 us (68%)
  matrix products  105 us (16%)
  local copies, waits for them, and re-layouts  80.4 us (13%)
  between operations  14.9 us (2%)
    reduce_scatter x1, waiting for transfers between devices, body(): lax.psum_scatter(partial_sums, 'rows', scatter_dimension=0, tiled=True)  181 us
    psum x1, waiting for transfers between devices, body(): lax.psum(jnp.dot(core_tile, coef_cols, precision=highest, preferred_eleme...  151 us
    scatter x1, local copies, waits for them, and re-layouts, body(): pivot_rank = jnp.full((rows_dev + 1,), total_rank, jnp.int32).at[target]....  60.3 us
    all_gather x1, waiting for transfers between devices, body(): dual_full = lax.all_gather(share[:, width:], 'rows', axis=0, tiled=True)  57.4 us
    dot_general x1, matrix products, body(): lax.dot_general(left_side, right_side, (((1,), (1,)), ((), ())), precisio...  33.5 us
    all_gather x1, waiting for transfers between devices, body(): coef_cols = lax.all_gather(coef_part, 'rank', axis=0, tiled=True)  23.1 us
    dot_general x1, matrix products, body(): jnp.dot(core_tile, coef_cols, precision=highest, preferred_element_type=j...  18.6 us
    dot_general x1, matrix products, body(): lax.dot_general(core_tile, dual_full, contract, precision=highest, prefer...  18.6 us
  transfers between devices with their start and end apart: 7, of which 6 were waited for; matrix products, arithmetic and copies ran while one was open for 23% of the time, Pallas kernels for 0%

commit v1 on v0

--- a/solution.py
+++ b/solution.py
@@ -1,7 +1,522 @@
+import functools
+
 import jax
 import jax.numpy as jnp
 from jax import lax
+from jax.experimental import pallas as pl
+from jax.experimental.pallas import tpu as pltpu
 from jax.sharding import PartitionSpec as P
+
+MESH = pl.DeviceIdType.MESH
+VMEM = pl.BlockSpec(memory_space=pltpu.VMEM)
+ANY = pl.BlockSpec(memory_space=pl.ANY)
+F32 = jnp.float32
+BF16 = jnp.bfloat16
+SUBS = 2
+NT = (((1,), (1,)), ((), ()))
+
+
+def halves(x):
+    high = x.astype(BF16)
+    low = (x - high.astype(F32)).astype(BF16)
+    return jnp.concatenate([high, low], axis=0)
+
+
+class Ring:
+    def __init__(self, n_rows):
+        self.n = n_rows // 2
+        row = lax.axis_index("rows")
+        self.row = row
+        self.rank = lax.axis_index("rank")
+        self.core = row % 2
+        chip = row // 2
+        odd = chip % 2
+        self.pos = (1 - odd) * (chip // 2) + odd * (self.n - 1 - chip // 2)
+        self.next = [self.device(self.pos + 1), self.device(self.pos - 1)]
+        self.sibling = (self.owner(self.pos, True), self.rank)
+        self.partner = (row, 1 - self.rank)
+
+    def owner(self, pos, other=False):
+        pos = (pos + 2 * self.n) % self.n
+        upper = (2 * pos) // self.n
+        chip = (1 - upper) * (2 * pos) + upper * (2 * (self.n - 1 - pos) + 1)
+        core = (1 - self.core) if other else self.core
+        return 2 * chip + core
+
+    def device(self, pos):
+        return (self.owner(pos), self.rank)
+
+    def enter(self, with_partner):
+        barrier = pltpu.get_barrier_semaphore()
+        peers = self.next + [self.sibling] + ([self.partner] if with_partner else [])
+        for peer in peers:
+            pl.semaphore_signal(barrier, inc=1, device_id=peer, device_id_type=MESH)
+        pl.semaphore_wait(barrier, len(peers))
+
+
+def remote(src, dst, send, recv, device):
+    return pltpu.make_async_remote_copy(
+        src_ref=src, dst_ref=dst, send_sem=send, recv_sem=recv, device_id=device, device_id_type=MESH
+    )
+
+
+class Gather:
+    def __init__(self, ring, buf, ring_sems, sib_sems):
+        self.ring, self.buf = ring, buf
+        self.rs, self.ss = ring_sems, sib_sems
+        self.half = buf.shape[1] // 2
+        self.sub = self.half // SUBS
+
+    def at(self, d, t):
+        return self.ring.pos - t if d == 0 else self.ring.pos + t
+
+    def part(self, owner, d, u):
+        return self.buf.at[owner, pl.ds(d * self.half + u * self.sub, self.sub)]
+
+    def hop(self, d, u, t):
+        ref = self.part(self.ring.owner(self.at(d, t)), d, u)
+        return remote(ref, ref, self.rs.at[0, d, u, t], self.rs.at[1, d, u, t], self.ring.next[d])
+
+    def hop_in(self, d, u, t):
+        ref = self.part(self.ring.owner(self.at(d, t + 1)), d, u)
+        return remote(ref, ref, self.rs.at[0, d, u, t], self.rs.at[1, d, u, t], self.ring.next[d])
+
+    def across(self, d, u, t):
+        ref = self.part(self.ring.owner(self.at(d, t)), d, u)
+        return remote(ref, ref, self.ss.at[0, d, u, t], self.ss.at[1, d, u, t], self.ring.sibling)
+
+    def across_in(self, d, u, t):
+        ref = self.part(self.ring.owner(self.at(d, t), True), d, u)
+        return remote(ref, ref, self.ss.at[0, d, u, t], self.ss.at[1, d, u, t], self.ring.sibling)
+
+    def step(self, t, first=False, last=False):
+        for u in range(SUBS):
+            for d in range(2):
+                if not first:
+                    self.hop_in(d, u, t - 1).wait_recv()
+                if not last:
+                    self.hop(d, u, t).start()
+                self.across(d, u, t).start()
+
+    def wait_across(self, t):
+        for u in range(SUBS):
+            for d in range(2):
+                self.across_in(d, u, t).wait_recv()
+
+    def mine(self, d, t):
+        return self.ring.owner(self.at(d, t))
+
+    def theirs(self, d, t):
+        return self.ring.owner(self.at(d, t), True)
+
+    def finish(self):
+        @pl.loop(0, self.ring.n)
+        def _(t):
+            for u in range(SUBS):
+                for d in range(2):
+                    self.across(d, u, t).wait_send()
+
+        @pl.loop(0, self.ring.n - 1)
+        def _(t):
+            for u in range(SUBS):
+                for d in range(2):
+                    self.hop(d, u, t).wait_send()
+
+
+class Scatter:
+    def __init__(self, ring, term, land, sib_in, sib_out, ring_sems, sib_sems):
+        self.ring, self.term = ring, term
+        self.land, self.sib_in, self.sib_out = land, sib_in, sib_out
+        self.rs, self.ss = ring_sems, sib_sems
+        self.sub = land.shape[2] // SUBS
+
+    def at(self, d, t):
+        return self.ring.pos - 1 - t if d == 0 else self.ring.pos + 1 + t
+
+    def across(self, d, t):
+        return remote(
+            self.sib_out.at[t, d], self.sib_in.at[t, d], self.ss.at[0, d, t], self.ss.at[1, d, t], self.ring.sibling
+        )
+
+    def rows(self, u):
+        return pl.ds(u * self.sub, self.sub)
+
+    def hop(self, d, u, t, first=False):
+        src = self.sib_in.at[0, d, self.rows(u)] if first else self.land.at[t - 1, d, self.rows(u)]
+        dst = self.land.at[t, d, self.rows(u)]
+        return remote(src, dst, self.rs.at[0, d, u, t], self.rs.at[1, d, u, t], self.ring.next[d])
+
+    def prepare(self, t):
+        for d in range(2):
+            self.sib_out[t, d] = self.term(self.ring.owner(self.at(d, t), True), d)
+            self.across(d, t).start()
+        own = [self.term(self.ring.owner(self.at(d, t)), d) for d in range(2)]
+        for d in range(2):
+            self.across(d, t).wait_recv()
+            self.sib_in[t, d] = self.sib_in[t, d] + own[d]
+
+    def start(self):
+        for u in range(SUBS):
+            for d in range(2):
+                self.hop(d, u, 0, True).start()
+
+    def step(self, t):
+        for u in range(SUBS):
+            for d in range(2):
+                into = self.land.at[t - 1, d, self.rows(u)]
+                remote(into, into, self.rs.at[0, d, u, t - 1], self.rs.at[1, d, u, t - 1], self.ring.next[d]).wait_recv()
+                self.land[t - 1, d, self.rows(u)] = self.land[t - 1, d, self.rows(u)] + self.sib_in[t, d, self.rows(u)]
+                self.hop(d, u, t).start()
+
+    def result(self, d):
+        last = self.ring.n - 1
+        for u in range(SUBS):
+            into = self.land.at[last - 1, d, self.rows(u)]
+            remote(
+                into, into, self.rs.at[0, d, u, last - 1], self.rs.at[1, d, u, last - 1], self.ring.next[d]
+            ).wait_recv()
+        return self.land[last - 1, d] + self.sib_in[last, d]
+
+    def finish(self):
+        for u in range(SUBS):
+            for d in range(2):
+                self.hop(d, u, 0, True).wait_send()
+
+        @pl.loop(1, self.ring.n - 1)
+        def _(t):
+            for u in range(SUBS):
+                for d in range(2):
+                    self.hop(d, u, t).wait_send()
+
+        @pl.loop(0, self.ring.n)
+        def _(t):
+            for d in range(2):
+                self.across(d, t).wait_send()
+
+
+def columns(owner, slim):
+    return pl.ds(pl.multiple_of(owner * slim, 128), slim)
+
+
+def sums_kernel(n_rows, left_ref, factor_ref, cols_ref, dual_ref, fac, land, sib_in, sib_out, swap, load, rs, ss, xs):
+    ring = Ring(n_rows)
+    bulk = pltpu.make_async_copy(factor_ref, fac, load.at[0])
+    bulk.start()
+    ring.enter(True)
+    bulk.wait()
+    width = left_ref.shape[0] // 2
+    slim = dual_ref.shape[1]
+
+    def term(owner, d):
+        return jnp.dot(
+            left_ref[d * width : (d + 1) * width, :], fac[:, columns(owner, slim)], preferred_element_type=F32
+        )
+
+    sums = Scatter(ring, term, land, sib_in, sib_out, rs, ss)
+    sums.prepare(0)
+    sums.start()
+    sums.prepare(1)
+
+    @pl.loop(1, ring.n - 1)
+    def _(t):
+        sums.step(t)
+        sums.prepare(t + 1)
+
+    swap[0] = sums.result(0)
+    move = remote(swap.at[0], swap.at[1], xs.at[0], xs.at[1], ring.partner)
+    move.start()
+    dual_ref[...] = sums.result(1)
+    cols_ref[ring.rank] = swap[0]
+    move.wait_recv()
+    cols_ref[1 - ring.rank] = swap[1]
+    move.wait_send()
+    sums.finish()
+
+
+def duals_kernel(n_rows, own_ref, core_ref, dual_ref, core, buf, acc, swap, load, rs, ss, xs):
+    ring = Ring(n_rows)
+    bulk = pltpu.make_async_copy(core_ref, core, load.at[0])
+    bulk.start()
+    buf[ring.row] = own_ref[...]
+    acc[...] = jnp.zeros_like(acc)
+    ring.enter(True)
+    slim = own_ref.shape[1]
+    gather = Gather(ring, buf, rs, ss)
+    half = gather.half
+
+    def consume(owner, d):
+        pair = halves(buf[owner, d * half : (d + 1) * half, :])
+        both = jnp.dot(pair, core[columns(owner, slim), :], preferred_element_type=F32)
+        both = both[:half] + both[half:]
+        for k in range(2):
+            acc[k, d * half : (d + 1) * half, :] += both[:, k * slim : (k + 1) * slim]
+
+    gather.step(0, first=True)
+    bulk.wait()
+    for d in range(2):
+        consume(gather.mine(d, 0), d)
+
+    @pl.loop(1, ring.n - 1)
+    def _(t):
+        gather.step(t)
+        gather.wait_across(t - 1)
+        for d in range(2):
+            consume(gather.theirs(d, t - 1), d)
+            consume(gather.mine(d, t), d)
+
+    gather.step(ring.n - 1, last=True)
+    gather.wait_across(ring.n - 2)
+    for d in range(2):
+        consume(gather.theirs(d, ring.n - 2), d)
+        consume(gather.mine(d, ring.n - 1), d)
+    gather.wait_across(ring.n - 1)
+    for d in range(2):
+        consume(gather.theirs(d, ring.n - 1), d)
+    move = remote(acc.at[1 - ring.rank], swap, xs.at[0], xs.at[1], ring.partner)
+    move.start()
+    move.wait_recv()
+    dual_ref[...] = acc[ring.rank] + swap[...]
+    move.wait_send()
+    gather.finish()
+
+
+def weights_kernel(
+    n_rows, cols_ref, own_ref, core_ref, duals_ref, weight_ref,
+    core, buf, pairs, land, sib_in, sib_out, load, grs, gss, rs, ss,
+):
+    ring = Ring(n_rows)
+    bulk = pltpu.make_async_copy(core_ref, core, load.at[0])
+    bulk.start()
+    buf[ring.row] = own_ref[...]
+    slim = own_ref.shape[1]
+    gather = Gather(ring, buf, grs, gss)
+    half = gather.half
+    for d in range(2):
+        for k in range(2):
+            pairs[d, :, k * slim : (k + 1) * slim] = halves(cols_ref[k, d * half : (d + 1) * half, :])
+    ring.enter(False)
+    gather.step(0, first=True)
+    bulk.wait()
+
+    def term(owner, d):
+        both = lax.dot_general(pairs[d], core[columns(owner, slim), :], NT, preferred_element_type=F32)
+        return both[:half] + both[half:]
+
+    sums = Scatter(ring, term, land, sib_in, sib_out, rs, ss)
+    sums.prepare(0)
+    sums.start()
+    sums.prepare(1)
+
+    @pl.loop(1, ring.n - 1)
+    def _(t):
+        gather.step(t)
+        sums.step(t)
+        sums.prepare(t + 1)
+        gather.wait_across(t - 1)
+
+    gather.step(ring.n - 1, last=True)
+    for d in range(2):
+        weight_ref[d * half : (d + 1) * half, :] = sums.result(d)
+    gather.wait_across(ring.n - 2)
+    gather.wait_across(ring.n - 1)
+    out = pltpu.make_async_copy(buf, duals_ref, load.at[1])
+    out.start()
+    gather.finish()
+    sums.finish()
+    out.wait()
+
+
+def spread_kernel(
+    n_rows, own_ref, duals_in, factor_ref, weights_ref, product_ref, fac, duals, buf, acc, swap, load, rs, ss, xs
+):
+    ring = Ring(n_rows)
+    bulk = pltpu.make_async_copy(factor_ref, fac, load.at[0])
+    bulk.start()
+    second = pltpu.make_async_copy(duals_in, duals, load.at[1])
+    second.start()
+    buf[ring.row] = own_ref[...]
+    acc[...] = jnp.zeros_like(acc)
+    ring.enter(True)
+    slim = own_ref.shape[1]
+    width = own_ref.shape[0]
+    gather = Gather(ring, buf, rs, ss)
+    tiles = 4
+    each = n_rows // tiles
+
+    def multiply(first):
+        @pl.loop(0, each)
+        def _(i):
+            owner = first * each + i
+            both = lax.dot_general(
+                fac[:, columns(owner, slim)], halves(duals[owner]), NT, preferred_element_type=F32
+            )
+            acc[...] += both[:, :width] + both[:, width:]
+
+    gather.step(0, first=True)
+    bulk.wait()
+    second.wait()
+    for i in range(tiles):
+        multiply(i)
+        if i + 1 < ring.n - 1:
+            gather.step(i + 1)
+    move = remote(acc, swap, xs.at[0], xs.at[1], ring.partner)
+    move.start()
+
+    @pl.loop(min(tiles + 1, ring.n - 1), ring.n - 1)
+    def _(t):
+        gather.step(t)
+
+    gather.step(ring.n - 1, last=True)
+
+    @pl.loop(0, ring.n)
+    def _(t):
+        gather.wait_across(t)
+
+    out = pltpu.make_async_copy(buf, weights_ref, load.at[2])
+    out.start()
+    move.wait_recv()
+    product_ref[...] = acc[...] + swap[...]
+    move.wait_send()
+    gather.finish()
+    out.wait()
+
+
+def outer_kernel(scale_ref, left_ref, rank_ref, weights_ref, duals_ref, out_ref):
+    first = lax.axis_index("rank") * (out_ref.shape[1] * pl.num_programs(0)) + pl.program_id(0) * out_ref.shape[1]
+    right = halves(jnp.concatenate([weights_ref[0], duals_ref[0]], axis=0))
+    scale = scale_ref[0]
+    rows = left_ref.shape[0]
+    tile = min(rows, 256)
+    for r in range(0, rows, tile):
+        total = jnp.dot(left_ref[r : r + tile, :], right, preferred_element_type=F32)
+        where = first + lax.broadcasted_iota(jnp.int32, total.shape, 1)
+        keep = where <= rank_ref[r : r + tile, :]
+        out_ref[r : r + tile, :] = jnp.where(keep, -total / scale, 0.0).astype(BF16)
+
+
+def sems(*shape):
+    return pltpu.SemaphoreType.DMA(shape)
+
+
+def params(n):
+    return pltpu.CompilerParams(collective_id=n, has_side_effects=True, vmem_limit_bytes=60 * 2**20)
+
+
+def shape_of(*shape):
+    return jax.ShapeDtypeStruct(shape, F32)
+
+
+def ranks_of_rows(pivots, first_row, rows_dev):
+    total = pivots.shape[0]
+    local = pivots - first_row
+    number = jnp.arange(1, total + 1, dtype=jnp.int32)
+    high = (local >> 7)[None, :] == jnp.arange(rows_dev // 128, dtype=jnp.int32)[:, None]
+    low = ((local & 127)[:, None] == jnp.arange(128, dtype=jnp.int32)[None, :]).astype(BF16)
+    upper = jnp.where(high, number >> 7, 0).astype(BF16)
+    lower = jnp.where(high, number & 127, 0).astype(BF16)
+    found = jnp.dot(jnp.concatenate([upper, lower], axis=0), low, preferred_element_type=F32)
+    found = found.astype(jnp.int32).reshape(2, rows_dev)
+    found = found[0] * 128 + found[1]
+    return jnp.where(found > 0, found - 1, total)
+
+
+def ring_body(factor, probes, cotangent, core_inverse, pivots, noise):
+    rows_dev, block_cols = factor.shape
+    width = probes.shape[1]
+    n_rows = lax.axis_size("rows")
+    slim = block_cols // n_rows
+    n = n_rows // 2
+    half = width // 2
+    scale = noise[0]
+    core_tile = core_inverse.reshape(block_cols, 2 * slim)
+    left = jnp.concatenate([probes.T, cotangent.T], axis=0)
+    ring_sem = sems(2, 2, SUBS, n)
+    sib_sem = sems(2, 2, n)
+    bucket = pltpu.VMEM((n_rows, width, slim), F32)
+    coef_cols, dual_in = pl.pallas_call(
+        functools.partial(sums_kernel, n_rows),
+        out_shape=(shape_of(2, width, slim), shape_of(width, slim)),
+        in_specs=[VMEM, ANY],
+        out_specs=(VMEM, VMEM),
+        scratch_shapes=[
+            pltpu.VMEM(factor.shape, BF16),
+            pltpu.VMEM((n - 1, 2, width, slim), F32),
+            pltpu.VMEM((n, 2, width, slim), F32),
+            pltpu.VMEM((n, 2, width, slim), F32),
+            pltpu.VMEM((2, width, slim), F32),
+            sems(1), ring_sem, sib_sem, sems(2),
+        ],
+        compiler_params=params(0),
+        name="sums",
+    )(left, factor)
+    dual_own = pl.pallas_call(
+        functools.partial(duals_kernel, n_rows),
+        out_shape=shape_of(width, slim),
+        in_specs=[VMEM, ANY],
+        out_specs=VMEM,
+        scratch_shapes=[
+            pltpu.VMEM(core_tile.shape, BF16),
+            bucket,
+            pltpu.VMEM((2, width, slim), F32),
+            pltpu.VMEM((width, slim), F32),
+            sems(1), ring_sem, ring_sem, sems(2),
+        ],
+        compiler_params=params(1),
+        name="duals",
+    )(dual_in, core_tile)
+    duals, weight_own = pl.pallas_call(
+        functools.partial(weights_kernel, n_rows),
+        out_shape=(shape_of(n_rows, width, slim), shape_of(width, slim)),
+        in_specs=[VMEM, VMEM, ANY],
+        out_specs=(ANY, VMEM),
+        scratch_shapes=[
+            pltpu.VMEM(core_tile.shape, BF16),
+            bucket,
+            pltpu.VMEM((2, width, 2 * slim), BF16),
+            pltpu.VMEM((n - 1, 2, half, slim), F32),
+            pltpu.VMEM((n, 2, half, slim), F32),
+            pltpu.VMEM((n, 2, half, slim), F32),
+            sems(2), ring_sem, ring_sem, ring_sem, sib_sem,
+        ],
+        compiler_params=params(2),
+        name="weights",
+    )(coef_cols, dual_own, core_tile)
+    weights, product = pl.pallas_call(
+        functools.partial(spread_kernel, n_rows),
+        out_shape=(shape_of(n_rows, width, slim), shape_of(rows_dev, width)),
+        in_specs=[VMEM, ANY, ANY],
+        out_specs=(ANY, VMEM),
+        scratch_shapes=[
+            pltpu.VMEM(factor.shape, BF16),
+            bucket,
+            bucket,
+            pltpu.VMEM((rows_dev, width), F32),
+            pltpu.VMEM((rows_dev, width), F32),
+            sems(3), ring_sem, ring_sem, sems(2),
+        ],
+        compiler_params=params(3),
+        name="spread",
+    )(weight_own, duals, factor)
+    probe_grad = ((cotangent.astype(F32) - product) / scale).astype(BF16)
+    pivot_rank = ranks_of_rows(pivots, lax.axis_index("rows") * rows_dev, rows_dev)
+    pair = jnp.concatenate([cotangent, probes, cotangent, probes], axis=1)
+    block = pl.BlockSpec((1, width, slim), lambda j: (j, 0, 0))
+    grads = pl.pallas_call(
+        outer_kernel,
+        grid=(n_rows,),
+        out_shape=jax.ShapeDtypeStruct(factor.shape, BF16),
+        in_specs=[
+            pl.BlockSpec(memory_space=pltpu.SMEM),
+            pl.BlockSpec((rows_dev, 4 * width), lambda j: (0, 0)),
+            pl.BlockSpec((rows_dev, 1), lambda j: (0, 0)),
+            block,
+            block,
+        ],
+        out_specs=pl.BlockSpec((rows_dev, slim), lambda j: (0, j)),
+        compiler_params=pltpu.CompilerParams(vmem_limit_bytes=40 * 2**20),
+        name="outer",
+    )(noise, pair, pivot_rank[:, None], weights, duals)
+    return probe_grad, grads
 
 
 def body(factor, probes, cotangent, core_inverse, pivots, noise):
@@ -73,8 +588,16 @@
         P(),
         P(),
     )
+    n_rows, n_rank = mesh.shape["rows"], mesh.shape["rank"]
+
+    def chosen(factor, probes, cotangent, core_inverse, pivots, noise):
+        slim = factor.shape[1] // n_rows
+        fits = n_rank == 2 and n_rows % 4 == 0 and slim % 128 == 0 and factor.shape[0] % 128 == 0
+        run = ring_body if fits and pivots.shape[0] <= 2**15 else body
+        return run(factor, probes, cotangent, core_inverse, pivots, noise)
+
     return jax.shard_map(
-        body,
+        chosen,
         mesh=mesh,
         in_specs=placed,
         out_specs=(P("rows", None), P("rows", "rank")),

time: 643 us -> 373 us (0.58)
  waiting for transfers between devices: 440 us -> 0 us
  Pallas kernels: 0 us -> 343 us
  matrix products: 105 us -> 2.34 us
  local copies, waits for them, and re-layouts: 80.4 us -> 20.6 us
  between operations: 14.9 us -> 1.49 us
    pallas_call x0 -> x5, Pallas kernels: none -> 343 us  [the longest x1 109 us: ring_body(): pl.pallas_call(functools.partial(sums_kernel, n_rows), out_shape=(shape_o...]
    reduce_scatter x2 -> x0, waiting for transfers between devices: 199 us -> none  [the longest x1 181 us: body(): lax.psum_scatter(partial_sums, 'rows', scatter_dimension=0, tiled=True)]
    psum x2 -> x0, waiting for transfers between devices: 160 us -> none  [the longest x1 151 us: body(): lax.psum(jnp.dot(core_tile, coef_cols, precision=highest, preferred_eleme...]
    dot_general x5 -> x1, matrix products: 105 us -> 2.34 us  [ranks_of_rows(): jnp.dot(jnp.concatenate([upper, lower], axis=0), low, preferred_element_t...]
    all_gather x3 -> x0, waiting for transfers between devices: 80.5 us -> none  [the longest x1 57.4 us: body(): dual_full = lax.all_gather(share[:, width:], 'rows', axis=0, tiled=True)]
    scatter x1 -> x0, local copies, waits for them, and re-layouts: 60.3 us -> none  [body(): pivot_rank = jnp.full((rows_dev + 1,), total_rank, jnp.int32).at[target]....]
    unnamed x9 -> x11, local copies, waits for them, and re-layouts: 17.9 us -> 20.4 us
  transfers between devices with their start and end apart: 7 -> 0, of which waited for: 6 -> 0; matrix products, arithmetic and copies ran while one was open for 23% -> 0% of each run, Pallas kernels for 0% -> 0%
where the time goes in v1:
time: 373 us; the launch traced here: 372 us
  Pallas kernels  343 us (92%)
  local copies, waits for them, and re-layouts  20.6 us (6%)
  other arithmetic  4.45 us (1%)
    pallas_call x1, Pallas kernels, ring_body(): pl.pallas_call(functools.partial(sums_kernel, n_rows), out_shape=(shape_o...  109 us
    pallas_call x1, Pallas kernels, ring_body(): pl.pallas_call(functools.partial(weights_kernel, n_rows), out_shape=(shap...  91.2 us
    pallas_call x1, Pallas kernels, ring_body(): pl.pallas_call(functools.partial(duals_kernel, n_rows), out_shape=shape_o...  60.8 us
    pallas_call x1, Pallas kernels, ring_body(): pl.pallas_call(functools.partial(spread_kernel, n_rows), out_shape=(shape...  58.1 us
    pallas_call x1, Pallas kernels, ring_body(): pl.pallas_call(outer_kernel, grid=(n_rows,), out_shape=jax.ShapeDtypeStru...  23.8 us
    unnamed x11, local copies, waits for them, and re-layouts  20.4 us

profile of v1, /device:TPU:0, one launch (start us, length us, event | category | flops | bytes accessed | tf_op | source)
XLA Modules:
  0.0 371.5 jit_solution(12137371613513241123)
XLA Ops:
  0.6 0.0 copy-start.1
  0.6 0.0 copy-start.2
  1.4 0.9 subtract_shift-right-arithmetic_fusion
  2.3 0.1 select_convert_fusion.1
  2.4 2.3 fusion.2
  4.7 0.2 copy.12.rank_ref
  5.0 0.0 copy-done.2
  5.0 0.2 copy.10
  5.2 0.0 copy-done.1
  5.2 0.2 copy.11
  5.4 1.0 pad_maximum_fusion.1.left_ref
  6.5 0.0 copy-start.3
  6.5 108.7 %sums.1 = (f32[2,256,512]{2,1,0:T(8,128)}, f32[256,512]{1,0:T(8,128)}) custom-call(bf16[512,1024]{1,0:T(8,128)(2,1)} %pad_maximum_fusion.1.left_ref, bf16[1024,8192]{1,0:T(8,128)(2,1)} %factor_ref.3), custom_call_target="tpu_custom_call" | custom-call | tf_op jit(solution)/shard_map/sums/pallas_call | solution.py:436
  115.1 0.0 copy-done.3
  115.1 0.3 pad_maximum_fusion.left_ref
  115.4 16.6 %copy.13 = bf16[1024,8,2,512]{3,1,2,0:T(8,128)(2,1)} copy(bf16[1024,8,2,512]{3,2,1,0:T(2,128)(2,1)} %bitcast.9) | data formatting | bytes 33554432
  132.0 60.8 %duals.1.own_ref = f32[256,512]{1,0:T(8,128)} custom-call(f32[256,512]{1,0:T(8,128)} %get-tuple-element.9.own_ref, bf16[8192,1024]{1,0:T(8,128)(2,1)} %bitcast.7), custom_call_target="tpu_custom_call" | custom-call | tf_op jit(solution)/shard_map/duals/pallas_call | solution.py:452
  192.9 91.2 %weights.1 = (f32[16,256,512]{2,1,0:T(8,128)}, f32[256,512]{1,0:T(8,128)}) custom-call(f32[2,256,512]{2,1,0:T(8,128)} %get-tuple-element.8.cols_ref, f32[256,512]{1,0:T(8,128)} %duals.1.own_ref, bf16[8192,1024]{1,0:T(8,128)(2,1)} %bitcast.8), custom_call_target="tpu_custom_call" | custom-call | tf_op jit(solution)/shard_map/weights/pallas_call | solution.py:467
  284.1 58.1 %spread.1 = (f32[16,256,512]{2,1,0:T(8,128)}, f32[1024,256]{1,0:T(8,128)}) custom-call(f32[256,512]{1,0:T(8,128)} %get-tuple-element.10.own_ref, f32[16,256,512]{2,1,0:T(8,128)} %get-tuple-element.11.duals_in.duals_ref, bf16[1024,8192]{1,0:T(8,128)(2,1)} %factor_ref.3), custom_call_target="tpu_custom_call" | custom-call | tf_op jit(solution)/shard_map/spread/pallas_call | solution.py:484
  342.2 2.2 divide_convert_fusion
  344.3 0.0 copy-start
  344.3 3.4 copy-done
  347.7 23.8 %outer.1 = bf16[1024,8192]{1,0:T(8,128)(2,1)} custom-call(f32[1]{0:T(128)} %copy.14.scale_ref, bf16[1024,1024]{1,0:T(8,128)(2,1)S(1)} %pad_maximum_fusion.left_ref, s32[1024,1]{1,0:T(8,128)S(1)} %copy.12.rank_ref, f32[16,256,512]{2,1,0:T(8,128)S(1)} %copy-done, f32[16,256,512]{2,1,0:T(8,128)} %get-tuple-element.11.duals_in.duals_ref), custom_call_target="tpu_custom_call" | custom-call | tf_op jit(solution)/shard_map/outer/pallas_call | solution.py:504
  (2 shorter events, 0.0 us)
Async XLA Ops:
  0.6 4.6 %copy-start.1 = (bf16[1024,256]{1,0:T(8,128)(2,1)S(1)}, bf16[1024,256]{1,0:T(8,128)(2,1)}, u32[]{:S(2)}) copy-start(bf16[1024,256]{1,0:T(8,128)(2,1)} %param.8) | copy-start | bytes 1572868
  0.6 4.3 %copy-start.2 = (bf16[1024,256]{1,0:T(8,128)(2,1)S(1)}, bf16[1024,256]{1,0:T(8,128)(2,1)}, u32[]{:S(2)}) copy-start(bf16[1024,256]{1,0:T(8,128)(2,1)} %param.7) | copy-start | bytes 1572868
  6.5 108.7 %copy-start.3 = (bf16[1024,256]{1,0:T(8,128)(2,1)S(1)}, bf16[1024,256]{1,0:T(8,128)(2,1)}, u32[]{:S(2)}) copy-start(bf16[1024,256]{1,0:T(8,128)(2,1)} %param.7) | copy-start | bytes 1572868
  344.3 3.4 copy-start

commit v2 on v1

--- a/solution.py
+++ b/solution.py
@@ -198,14 +198,51 @@
     return pl.ds(pl.multiple_of(owner * slim, 128), slim)
 
 
-def sums_kernel(n_rows, left_ref, factor_ref, cols_ref, dual_ref, fac, land, sib_in, sib_out, swap, load, rs, ss, xs):
+def sums_kernel(
+    n_rows, left_ref, factor_ref, core_ref, coef_ref, dual_ref, tile_ref,
+    fac, land, sib_in, sib_out, raw, flat, load, raws, flats, rs, ss,
+):
     ring = Ring(n_rows)
-    bulk = pltpu.make_async_copy(factor_ref, fac, load.at[0])
-    bulk.start()
-    ring.enter(True)
-    bulk.wait()
-    width = left_ref.shape[0] // 2
     slim = dual_ref.shape[1]
+    width = dual_ref.shape[0]
+    n = ring.n
+    deep = raw.shape[1]
+
+    def piece(offset, slot):
+        chip = ring.owner(ring.pos + offset) // 2
+        cols = columns(chip, 2 * slim)
+        return pltpu.make_async_copy(factor_ref.at[:, cols], fac.at[:, cols], load.at[slot])
+
+    order = [-1, 1] + [o for i in range(2, n // 2) for o in (-i, i)] + [n // 2, 0]
+    pieces = [piece(offset, slot) for slot, offset in enumerate(order)]
+    for copy in pieces:
+        copy.start()
+
+    def fetch(t):
+        rows = pl.ds(pl.multiple_of(t * deep, 16), deep)
+        return pltpu.make_async_copy(core_ref.at[rows], raw.at[t % 2], raws.at[t % 2])
+
+    def keep(t):
+        rows = pl.ds(pl.multiple_of(t * deep, 16), deep)
+        return pltpu.make_async_copy(flat.at[t % 2], tile_ref.at[rows], flats.at[t % 2])
+
+    def flatten(t, first=False, last=False):
+        fetch(t).wait()
+        if not last:
+            fetch(t + 1).start()
+        if not first:
+            keep(t - 1).wait()
+
+        @pl.loop(0, deep // 32)
+        def _(i):
+            rows = pl.ds(pl.multiple_of(i * 32, 32), 32)
+            for k in range(2):
+                flat[t % 2, rows, k * slim : (k + 1) * slim] = raw[t % 2, rows, k, :]
+
+        keep(t).start()
+
+    fetch(0).start()
+    ring.enter(False)
 
     def term(owner, d):
         return jnp.dot(
@@ -213,35 +250,39 @@
         )
 
     sums = Scatter(ring, term, land, sib_in, sib_out, rs, ss)
+    pieces[0].wait()
+    pieces[1].wait()
     sums.prepare(0)
     sums.start()
+    for copy in pieces[2:]:
+        copy.wait()
     sums.prepare(1)
-
-    @pl.loop(1, ring.n - 1)
+    flatten(0, first=True)
+
+    @pl.loop(1, n - 1)
     def _(t):
         sums.step(t)
         sums.prepare(t + 1)
-
-    swap[0] = sums.result(0)
-    move = remote(swap.at[0], swap.at[1], xs.at[0], xs.at[1], ring.partner)
-    move.start()
+        flatten(t)
+
+    flatten(n - 1, last=True)
+    coef_ref[...] = sums.result(0)
     dual_ref[...] = sums.result(1)
-    cols_ref[ring.rank] = swap[0]
-    move.wait_recv()
-    cols_ref[1 - ring.rank] = swap[1]
-    move.wait_send()
+    keep(n - 1).wait()
     sums.finish()
 
 
-def duals_kernel(n_rows, own_ref, core_ref, dual_ref, core, buf, acc, swap, load, rs, ss, xs):
+def mix_kernel(
+    n_rows, coef_ref, own_ref, core_ref, dual_ref, weight_ref,
+    core, buf, acc, swap, coefs, pairs, land, sib_in, sib_out, load, grs, gss, rs, ss, xs,
+):
     ring = Ring(n_rows)
     bulk = pltpu.make_async_copy(core_ref, core, load.at[0])
     bulk.start()
     buf[ring.row] = own_ref[...]
     acc[...] = jnp.zeros_like(acc)
-    ring.enter(True)
     slim = own_ref.shape[1]
-    gather = Gather(ring, buf, rs, ss)
+    gather = Gather(ring, buf, grs, gss)
     half = gather.half
 
     def consume(owner, d):
@@ -251,14 +292,34 @@
         for k in range(2):
             acc[k, d * half : (d + 1) * half, :] += both[:, k * slim : (k + 1) * slim]
 
+    def term(owner, d):
+        rows = columns(owner, slim)
+        both = lax.dot_general(pairs[0, d], core[rows, :slim], NT, preferred_element_type=F32)
+        both = both + lax.dot_general(pairs[1, d], core[rows, slim:], NT, preferred_element_type=F32)
+        return both[:half] + both[half:]
+
+    ring.enter(True)
+    other = remote(coef_ref, coefs, xs.at[0], xs.at[1], ring.partner)
+    other.start()
     gather.step(0, first=True)
+    for d in range(2):
+        pairs[ring.rank, d] = halves(coef_ref[d * half : (d + 1) * half, :])
     bulk.wait()
     for d in range(2):
         consume(gather.mine(d, 0), d)
+    other.wait_recv()
+    for d in range(2):
+        pairs[1 - ring.rank, d] = halves(coefs[d * half : (d + 1) * half, :])
+    sums = Scatter(ring, term, land, sib_in, sib_out, rs, ss)
+    sums.prepare(0)
+    sums.start()
+    sums.prepare(1)
 
     @pl.loop(1, ring.n - 1)
     def _(t):
         gather.step(t)
+        sums.step(t)
+        sums.prepare(t + 1)
         gather.wait_across(t - 1)
         for d in range(2):
             consume(gather.theirs(d, t - 1), d)
@@ -272,113 +333,86 @@
     gather.wait_across(ring.n - 1)
     for d in range(2):
         consume(gather.theirs(d, ring.n - 1), d)
-    move = remote(acc.at[1 - ring.rank], swap, xs.at[0], xs.at[1], ring.partner)
+    move = remote(acc.at[1 - ring.rank], swap, xs.at[2], xs.at[3], ring.partner)
     move.start()
+    for d in range(2):
+        weight_ref[d * half : (d + 1) * half, :] = sums.result(d)
     move.wait_recv()
     dual_ref[...] = acc[ring.rank] + swap[...]
     move.wait_send()
-    gather.finish()
-
-
-def weights_kernel(
-    n_rows, cols_ref, own_ref, core_ref, duals_ref, weight_ref,
-    core, buf, pairs, land, sib_in, sib_out, load, grs, gss, rs, ss,
-):
-    ring = Ring(n_rows)
-    bulk = pltpu.make_async_copy(core_ref, core, load.at[0])
-    bulk.start()
-    buf[ring.row] = own_ref[...]
-    slim = own_ref.shape[1]
-    gather = Gather(ring, buf, grs, gss)
-    half = gather.half
-    for d in range(2):
-        for k in range(2):
-            pairs[d, :, k * slim : (k + 1) * slim] = halves(cols_ref[k, d * half : (d + 1) * half, :])
-    ring.enter(False)
-    gather.step(0, first=True)
-    bulk.wait()
-
-    def term(owner, d):
-        both = lax.dot_general(pairs[d], core[columns(owner, slim), :], NT, preferred_element_type=F32)
-        return both[:half] + both[half:]
-
-    sums = Scatter(ring, term, land, sib_in, sib_out, rs, ss)
-    sums.prepare(0)
-    sums.start()
-    sums.prepare(1)
-
-    @pl.loop(1, ring.n - 1)
-    def _(t):
-        gather.step(t)
-        sums.step(t)
-        sums.prepare(t + 1)
-        gather.wait_across(t - 1)
-
-    gather.step(ring.n - 1, last=True)
-    for d in range(2):
-        weight_ref[d * half : (d + 1) * half, :] = sums.result(d)
-    gather.wait_across(ring.n - 2)
-    gather.wait_across(ring.n - 1)
-    out = pltpu.make_async_copy(buf, duals_ref, load.at[1])
-    out.start()
+    other.wait_send()
     gather.finish()
     sums.finish()
-    out.wait()
 
 
 def spread_kernel(
-    n_rows, own_ref, duals_in, factor_ref, weights_ref, product_ref, fac, duals, buf, acc, swap, load, rs, ss, xs
+    n_rows, dual_ref, weight_ref, factor_ref, duals_ref, weights_ref, product_ref,
+    fac, dbuf, wbuf, load, outs, drs, dss, wrs, wss,
 ):
     ring = Ring(n_rows)
     bulk = pltpu.make_async_copy(factor_ref, fac, load.at[0])
     bulk.start()
-    second = pltpu.make_async_copy(duals_in, duals, load.at[1])
-    second.start()
-    buf[ring.row] = own_ref[...]
-    acc[...] = jnp.zeros_like(acc)
-    ring.enter(True)
-    slim = own_ref.shape[1]
-    width = own_ref.shape[0]
-    gather = Gather(ring, buf, rs, ss)
-    tiles = 4
-    each = n_rows // tiles
-
-    def multiply(first):
-        @pl.loop(0, each)
-        def _(i):
-            owner = first * each + i
-            both = lax.dot_general(
-                fac[:, columns(owner, slim)], halves(duals[owner]), NT, preferred_element_type=F32
-            )
-            acc[...] += both[:, :width] + both[:, width:]
-
-    gather.step(0, first=True)
+    dbuf[ring.row] = dual_ref[...]
+    wbuf[ring.row] = weight_ref[...]
+    product_ref[...] = jnp.zeros_like(product_ref)
+    slim = dual_ref.shape[1]
+    duals = Gather(ring, dbuf, drs, dss)
+    weights = Gather(ring, wbuf, wrs, wss)
+    half = duals.half
+
+    def out(which, other, d, t):
+        buf, ref = ((dbuf, duals_ref), (wbuf, weights_ref))[which]
+        owner = duals.theirs(d, t) if other else duals.mine(d, t)
+        rows = pl.ds(d * half, half)
+        return pltpu.make_async_copy(buf.at[owner, rows], ref.at[owner, rows], outs.at[which, other, d, t])
+
+    def consume(owner, d):
+        right = halves(dbuf[owner, d * half : (d + 1) * half, :])
+        both = lax.dot_general(fac[:, columns(owner, slim)], right, NT, preferred_element_type=F32)
+        product_ref[:, d * half : (d + 1) * half] += both[:, :half] + both[:, half:]
+
+    def use(other, t):
+        for d in range(2):
+            out(0, other, d, t).start()
+            out(1, other, d, t).start()
+        for d in range(2):
+            consume(duals.theirs(d, t) if other else duals.mine(d, t), d)
+
+    def crossed(t):
+        duals.wait_across(t)
+        weights.wait_across(t)
+
+    ring.enter(False)
+    duals.step(0, first=True)
+    weights.step(0, first=True)
     bulk.wait()
-    second.wait()
-    for i in range(tiles):
-        multiply(i)
-        if i + 1 < ring.n - 1:
-            gather.step(i + 1)
-    move = remote(acc, swap, xs.at[0], xs.at[1], ring.partner)
-    move.start()
-
-    @pl.loop(min(tiles + 1, ring.n - 1), ring.n - 1)
+    use(0, 0)
+
+    @pl.loop(1, ring.n - 1)
     def _(t):
-        gather.step(t)
-
-    gather.step(ring.n - 1, last=True)
+        duals.step(t)
+        weights.step(t)
+        crossed(t - 1)
+        use(1, t - 1)
+        use(0, t)
+
+    duals.step(ring.n - 1, last=True)
+    weights.step(ring.n - 1, last=True)
+    crossed(ring.n - 2)
+    use(1, ring.n - 2)
+    use(0, ring.n - 1)
+    crossed(ring.n - 1)
+    use(1, ring.n - 1)
 
     @pl.loop(0, ring.n)
     def _(t):
-        gather.wait_across(t)
-
-    out = pltpu.make_async_copy(buf, weights_ref, load.at[2])
-    out.start()
-    move.wait_recv()
-    product_ref[...] = acc[...] + swap[...]
-    move.wait_send()
-    gather.finish()
-    out.wait()
+        for which in range(2):
+            for other in range(2):
+                for d in range(2):
+                    out(which, other, d, t).wait()
+
+    duals.finish()
+    weights.finish()
 
 
 def outer_kernel(scale_ref, left_ref, rank_ref, weights_ref, duals_ref, out_ref):
@@ -428,75 +462,68 @@
     n = n_rows // 2
     half = width // 2
     scale = noise[0]
-    core_tile = core_inverse.reshape(block_cols, 2 * slim)
     left = jnp.concatenate([probes.T, cotangent.T], axis=0)
+    deep = block_cols // n
     ring_sem = sems(2, 2, SUBS, n)
     sib_sem = sems(2, 2, n)
     bucket = pltpu.VMEM((n_rows, width, slim), F32)
-    coef_cols, dual_in = pl.pallas_call(
+    block = pltpu.VMEM((width, slim), F32)
+    coef_own, dual_in, core_tile = pl.pallas_call(
         functools.partial(sums_kernel, n_rows),
-        out_shape=(shape_of(2, width, slim), shape_of(width, slim)),
-        in_specs=[VMEM, ANY],
-        out_specs=(VMEM, VMEM),
+        out_shape=(
+            shape_of(width, slim),
+            shape_of(width, slim),
+            jax.ShapeDtypeStruct((block_cols, 2 * slim), BF16),
+        ),
+        in_specs=[VMEM, ANY, ANY],
+        out_specs=(VMEM, VMEM, ANY),
         scratch_shapes=[
             pltpu.VMEM(factor.shape, BF16),
             pltpu.VMEM((n - 1, 2, width, slim), F32),
             pltpu.VMEM((n, 2, width, slim), F32),
             pltpu.VMEM((n, 2, width, slim), F32),
-            pltpu.VMEM((2, width, slim), F32),
-            sems(1), ring_sem, sib_sem, sems(2),
+            pltpu.VMEM((2, deep, 2, slim), BF16),
+            pltpu.VMEM((2, deep, 2 * slim), BF16),
+            sems(n), sems(2), sems(2), ring_sem, sib_sem,
         ],
         compiler_params=params(0),
         name="sums",
-    )(left, factor)
-    dual_own = pl.pallas_call(
-        functools.partial(duals_kernel, n_rows),
-        out_shape=shape_of(width, slim),
-        in_specs=[VMEM, ANY],
-        out_specs=VMEM,
+    )(left, factor, core_inverse)
+    dual_own, weight_own = pl.pallas_call(
+        functools.partial(mix_kernel, n_rows),
+        out_shape=(shape_of(width, slim), shape_of(width, slim)),
+        in_specs=[VMEM, VMEM, ANY],
+        out_specs=(VMEM, VMEM),
         scratch_shapes=[
             pltpu.VMEM(core_tile.shape, BF16),
             bucket,
             pltpu.VMEM((2, width, slim), F32),
-            pltpu.VMEM((width, slim), F32),
-            sems(1), ring_sem, ring_sem, sems(2),
-        ],
-        compiler_params=params(1),
-        name="duals",
-    )(dual_in, core_tile)
-    duals, weight_own = pl.pallas_call(
-        functools.partial(weights_kernel, n_rows),
-        out_shape=(shape_of(n_rows, width, slim), shape_of(width, slim)),
-        in_specs=[VMEM, VMEM, ANY],
-        out_specs=(ANY, VMEM),
-        scratch_shapes=[
-            pltpu.VMEM(core_tile.shape, BF16),
-            bucket,
-            pltpu.VMEM((2, width, 2 * slim), BF16),
+            block,
+            block,
+            pltpu.VMEM((2, 2, width, slim), BF16),
             pltpu.VMEM((n - 1, 2, half, slim), F32),
             pltpu.VMEM((n, 2, half, slim), F32),
             pltpu.VMEM((n, 2, half, slim), F32),
-            sems(2), ring_sem, ring_sem, ring_sem, sib_sem,
+            sems(1), ring_sem, ring_sem, ring_sem, sib_sem, sems(4),
         ],
-        compiler_params=params(2),
-        name="weights",
-    )(coef_cols, dual_own, core_tile)
-    weights, product = pl.pallas_call(
+        compiler_params=params(1),
+        name="mix",
+    )(coef_own, dual_in, core_tile)
+    duals, weights, product = pl.pallas_call(
         functools.partial(spread_kernel, n_rows),
-        out_shape=(shape_of(n_rows, width, slim), shape_of(rows_dev, width)),
-        in_specs=[VMEM, ANY, ANY],
-        out_specs=(ANY, VMEM),
+        out_shape=(shape_of(n_rows, width, slim), shape_of(n_rows, width, slim), shape_of(rows_dev, width)),
+        in_specs=[VMEM, VMEM, ANY],
+        out_specs=(ANY, ANY, VMEM),
         scratch_shapes=[
             pltpu.VMEM(factor.shape, BF16),
             bucket,
             bucket,
-            pltpu.VMEM((rows_dev, width), F32),
-            pltpu.VMEM((rows_dev, width), F32),
-            sems(3), ring_sem, ring_sem, sems(2),
+            sems(1), sems(2, 2, 2, n), ring_sem, ring_sem, ring_sem, ring_sem,
         ],
-        compiler_params=params(3),
+        compiler_params=params(2),
         name="spread",
-    )(weight_own, duals, factor)
+    )(dual_own, weight_own, factor)
+    product = product + lax.ppermute(product, "rank", [(0, 1), (1, 0)])
     probe_grad = ((cotangent.astype(F32) - product) / scale).astype(BF16)
     pivot_rank = ranks_of_rows(pivots, lax.axis_index("rows") * rows_dev, rows_dev)
     pair = jnp.concatenate([cotangent, probes, cotangent, probes], axis=1)
@@ -513,7 +540,12 @@
             block,
         ],
         out_specs=pl.BlockSpec((rows_dev, slim), lambda j: (0, j)),
-        compiler_params=pltpu.CompilerParams(vmem_limit_bytes=40 * 2**20),
+        compiler_params=pltpu.CompilerParams(vmem_limit_bytes=60 * 2**20),
+        cost_estimate=pl.CostEstimate(
+            flops=8 * rows_dev * width * block_cols,
+            bytes_accessed=2 * rows_dev * block_cols + 8 * width * block_cols,
+            transcendentals=0,
+        ),
         name="outer",
     )(noise, pair, pivot_rank[:, None], weights, duals)
     return probe_grad, grads
@@ -592,7 +624,7 @@
 
     def chosen(factor, probes, cotangent, core_inverse, pivots, noise):
         slim = factor.shape[1] // n_rows
-        fits = n_rank == 2 and n_rows % 4 == 0 and slim % 128 == 0 and factor.shape[0] % 128 == 0
+        fits = n_rank == 2 and n_rows % 4 == 0 and n_rows >= 8 and slim % 128 == 0 and factor.shape[0] % 128 == 0
         run = ring_body if fits and pivots.shape[0] <= 2**15 else body
         return run(factor, probes, cotangent, core_inverse, pivots, noise)
 

time: 373 us -> 331 us (0.89)
  Pallas kernels: 343 us -> 318 us
  local copies, waits for them, and re-layouts: 20.6 us -> 3.56 us
    pallas_call x2 -> x1, Pallas kernels: 152 us -> 107 us  [ring_body(): pl.pallas_call(functools.partial(mix_kernel, n_rows), out_shape=(shape_of...]
    pallas_call x1, Pallas kernels: 58.1 us -> 90.3 us  [ring_body(): pl.pallas_call(functools.partial(spread_kernel, n_rows), out_shape=(shape...]
    unnamed x11 -> x10, local copies, waits for them, and re-layouts: 20.4 us -> 2.52 us
    pallas_call x1, Pallas kernels: 109 us -> 94.7 us  [ring_body(): pl.pallas_call(functools.partial(sums_kernel, n_rows), out_shape=(shape_o...]
  transfers between devices with their start and end apart: 0 -> 1, of which waited for: 0 -> 0; matrix products, arithmetic and copies ran while one was open for 0% -> 2% of each run, Pallas kernels for 0% -> 8%
where the time goes in v2:
time: 331 us
  Pallas kernels  318 us (96%)
  other arithmetic  3.79 us (1%)
  local copies, waits for them, and re-layouts  3.56 us (1%)
    pallas_call x1, Pallas kernels, ring_body(): pl.pallas_call(functools.partial(mix_kernel, n_rows), out_shape=(shape_of...  107 us
    pallas_call x1, Pallas kernels, ring_body(): pl.pallas_call(functools.partial(sums_kernel, n_rows), out_shape=(shape_o...  94.7 us
    pallas_call x1, Pallas kernels, ring_body(): pl.pallas_call(functools.partial(spread_kernel, n_rows), out_shape=(shape...  90.3 us
    pallas_call x1, Pallas kernels, ring_body(): pl.pallas_call(outer_kernel, grid=(n_rows,), out_shape=jax.ShapeDtypeStru...  26.3 us
  transfers between devices with their start and end apart: 1, of which 0 were waited for; matrix products, arithmetic and copies ran while one was open for 2% of the time, Pallas kernels for 8%

profile of v2, /device:TPU:0, one launch (start us, length us, event | category | flops | bytes accessed | tf_op | source)
XLA Modules:
  0.0 330.5 jit_solution(1151409625424946055)
XLA Ops:
  0.6 1.2 copy.11
  1.9 1.2 copy.10
  3.1 1.0 pad_maximum_fusion.1.left_ref
  4.2 94.7 %sums.1 = (f32[256,512]{1,0:T(8,128)}, f32[256,512]{1,0:T(8,128)}, bf16[8192,1024]{1,0:T(8,128)(2,1)}) custom-call(bf16[512,1024]{1,0:T(8,128)(2,1)} %pad_maximum_fusion.1.left_ref, bf16[1024,8192]{1,0:T(8,128)(2,1)} %factor_ref.3, bf16[8192,2,512]{2,1,0:T(2,128)(2,1)} %core_ref.1), custom_call_target="tpu_custom_call" | custom-call | tf_op jit(solution)/shard_map/sums/pallas_call | solution.py:471
  98.9 107.1 %mix.1 = (f32[256,512]{1,0:T(8,128)}, f32[256,512]{1,0:T(8,128)}) custom-call(f32[256,512]{1,0:T(8,128)} %get-tuple-element.10.coef_ref, f32[256,512]{1,0:T(8,128)} %get-tuple-element.11.own_ref, bf16[8192,1024]{1,0:T(8,128)(2,1)} %get-tuple-element.12.core_ref), custom_call_target="tpu_custom_call" | custom-call | tf_op jit(solution)/shard_map/mix/pallas_call | solution.py:492
  206.0 0.0 copy-start
  206.0 0.0 copy-start.1
  206.0 0.0 copy-start.3
  206.0 90.3 %spread.1 = (f32[16,256,512]{2,1,0:T(8,128)}, f32[16,256,512]{2,1,0:T(8,128)}, f32[1024,256]{1,0:T(8,128)}) custom-call(f32[256,512]{1,0:T(8,128)} %get-tuple-element.13.dual_ref, f32[256,512]{1,0:T(8,128)} %get-tuple-element.14.weight_ref, bf16[1024,8192]{1,0:T(8,128)(2,1)} %factor_ref.3), custom_call_target="tpu_custom_call" | custom-call | tf_op jit(solution)/shard_map/spread/pallas_call | solution.py:512
  296.3 1.1 collective-permute-start
  297.4 0.0 copy-done
  297.4 0.0 copy-done.1
  297.4 1.6 pad_maximum_fusion.left_ref
  299.7 0.0 copy-done.3
  299.7 0.1 select_convert_fusion.1
  299.8 2.3 fusion.2
  302.2 1.0 copy.12.rank_ref
  303.2 0.0 copy-start.2
  303.2 26.3 %outer.1 = bf16[1024,8192]{1,0:T(8,128)(2,1)} custom-call(f32[1]{0:T(128)} %copy.13.scale_ref, bf16[1024,1024]{1,0:T(8,128)(2,1)} %pad_maximum_fusion.left_ref, s32[1024,1]{1,0:T(8,128)} %copy.12.rank_ref, f32[16,256,512]{2,1,0:T(8,128)} %get-tuple-element.16.weights_ref, f32[16,256,512]{2,1,0:T(8,128)} %get-tuple-element.17.duals_ref), custom_call_target="tpu_custom_call" | custom-call | flops 17179869184 | bytes 33554432 | tf_op jit(solution)/shard_map/outer/pallas_call | solution.py:531
  329.5 0.0 collective-permute-done
  329.5 0.0 copy-done.2
  329.5 1.0 divide_convert_fusion
  (3 shorter events, 0.0 us)
Async XLA Ops:
  206.0 91.4 %copy-start = (bf16[1024,256]{1,0:T(8,128)(2,1)S(1)}, bf16[1024,256]{1,0:T(8,128)(2,1)}, u32[]{:S(2)}) copy-start(bf16[1024,256]{1,0:T(8,128)(2,1)} %param.8) | copy-start | bytes 1572868
  206.0 91.4 %copy-start.1 = (bf16[1024,256]{1,0:T(8,128)(2,1)S(1)}, bf16[1024,256]{1,0:T(8,128)(2,1)}, u32[]{:S(2)}) copy-start(bf16[1024,256]{1,0:T(8,128)(2,1)} %param.7) | copy-start | bytes 1572868
  206.0 93.7 %copy-start.3 = (s32[16384]{0:T(1024)S(1)}, s32[16384]{0:T(1024)}, u32[]{:S(2)}) copy-start(s32[16384]{0:T(1024)} %param.10) | copy-start | bytes 196612
  296.3 33.2 %collective-permute-start = (f32[1024,256]{1,0:T(8,128)}, f32[1024,256]{1,0:T(8,128)S(1)}, u32[]{:S(2)}, u32[]{:S(2)}) collective-permute-start(f32[1024,256]{1,0:T(8,128)} %get-tuple-element.15), channel_id=1, source_target_pairs={{0,1},{1,0},{2,3},{3,2},{4,5},{5,4},{6,7},{7,6},{8,9},{9,8},{10,11... | collective-permute-start | bytes 3145736 | tf_op jit(solution)/shard_map/ppermute | solution.py:526
  303.2 26.3 %copy-start.2 = (f32[1024,256]{1,0:T(8,128)S(1)}, f32[1024,256]{1,0:T(8,128)}, u32[]{:S(2)}) copy-start(f32[1024,256]{1,0:T(8,128)} %get-tuple-element.15) | copy-start | bytes 3145732

commit v3 on v2

--- a/solution.py
+++ b/solution.py
@@ -318,12 +318,12 @@
     @pl.loop(1, ring.n - 1)
     def _(t):
         gather.step(t)
-        sums.step(t)
-        sums.prepare(t + 1)
         gather.wait_across(t - 1)
         for d in range(2):
             consume(gather.theirs(d, t - 1), d)
             consume(gather.mine(d, t), d)
+        sums.step(t)
+        sums.prepare(t + 1)
 
     gather.step(ring.n - 1, last=True)
     gather.wait_across(ring.n - 2)
@@ -391,9 +391,9 @@
     @pl.loop(1, ring.n - 1)
     def _(t):
         duals.step(t)
-        weights.step(t)
         crossed(t - 1)
         use(1, t - 1)
+        weights.step(t)
         use(0, t)
 
     duals.step(ring.n - 1, last=True)
@@ -425,7 +425,7 @@
         total = jnp.dot(left_ref[r : r + tile, :], right, preferred_element_type=F32)
         where = first + lax.broadcasted_iota(jnp.int32, total.shape, 1)
         keep = where <= rank_ref[r : r + tile, :]
-        out_ref[r : r + tile, :] = jnp.where(keep, -total / scale, 0.0).astype(BF16)
+        out_ref[r : r + tile, :] = jnp.where(keep, total * scale, 0.0).astype(BF16)
 
 
 def sems(*shape):
@@ -547,7 +547,7 @@
             transcendentals=0,
         ),
         name="outer",
-    )(noise, pair, pivot_rank[:, None], weights, duals)
+    )(-1.0 / noise, pair, pivot_rank[:, None], weights, duals)
     return probe_grad, grads
 
 

time: 331 us -> 331 us (level)
  no operation moved by 1% of the time
where the time goes in v3:
time: 331 us; the launch traced here: 330 us
  Pallas kernels  318 us (96%)
  other arithmetic  3.79 us (1%)
  local copies, waits for them, and re-layouts  3.56 us (1%)
    pallas_call x1, Pallas kernels, ring_body(): pl.pallas_call(functools.partial(mix_kernel, n_rows), out_shape=(shape_of...  107 us
    pallas_call x1, Pallas kernels, ring_body(): pl.pallas_call(functools.partial(sums_kernel, n_rows), out_shape=(shape_o...  94.7 us
    pallas_call x1, Pallas kernels, ring_body(): pl.pallas_call(functools.partial(spread_kernel, n_rows), out_shape=(shape...  90.3 us
    pallas_call x1, Pallas kernels, ring_body(): pl.pallas_call(outer_kernel, grid=(n_rows,), out_shape=jax.ShapeDtypeStru...  26.1 us
  transfers between devices with their start and end apart: 1, of which 0 were waited for; matrix products, arithmetic and copies ran while one was open for 2% of the time, Pallas kernels for 8%

profile of v3, /device:TPU:0, one launch (start us, length us, event | category | flops | bytes accessed | tf_op | source)
XLA Modules:
  0.0 330.4 jit_solution(4621443765336537197)
XLA Ops:
  0.6 1.2 copy.11
  1.9 1.2 copy.10
  3.1 1.0 pad_maximum_fusion.1.left_ref
  4.2 94.7 %sums.1 = (f32[256,512]{1,0:T(8,128)}, f32[256,512]{1,0:T(8,128)}, bf16[8192,1024]{1,0:T(8,128)(2,1)}) custom-call(bf16[512,1024]{1,0:T(8,128)(2,1)} %pad_maximum_fusion.1.left_ref, bf16[1024,8192]{1,0:T(8,128)(2,1)} %factor_ref.3, bf16[8192,2,512]{2,1,0:T(2,128)(2,1)} %core_ref.1), custom_call_target="tpu_custom_call" | custom-call | tf_op jit(solution)/shard_map/sums/pallas_call | solution.py:471
  98.9 107.1 %mix.1 = (f32[256,512]{1,0:T(8,128)}, f32[256,512]{1,0:T(8,128)}) custom-call(f32[256,512]{1,0:T(8,128)} %get-tuple-element.10.coef_ref, f32[256,512]{1,0:T(8,128)} %get-tuple-element.11.own_ref, bf16[8192,1024]{1,0:T(8,128)(2,1)} %get-tuple-element.12.core_ref), custom_call_target="tpu_custom_call" | custom-call | tf_op jit(solution)/shard_map/mix/pallas_call | solution.py:492
  206.0 0.0 copy-start
  206.0 0.0 copy-start.1
  206.0 0.0 copy-start.3
  206.0 90.3 %spread.1 = (f32[16,256,512]{2,1,0:T(8,128)}, f32[16,256,512]{2,1,0:T(8,128)}, f32[1024,256]{1,0:T(8,128)}) custom-call(f32[256,512]{1,0:T(8,128)} %get-tuple-element.13.dual_ref, f32[256,512]{1,0:T(8,128)} %get-tuple-element.14.weight_ref, bf16[1024,8192]{1,0:T(8,128)(2,1)} %factor_ref.3), custom_call_target="tpu_custom_call" | custom-call | tf_op jit(solution)/shard_map/spread/pallas_call | solution.py:512
  296.3 1.1 collective-permute-start
  297.4 0.0 copy-done
  297.4 0.0 copy-done.1
  297.4 1.6 pad_maximum_fusion.left_ref
  299.7 0.0 copy-done.3
  299.7 0.1 select_convert_fusion.1
  299.8 2.3 fusion.2
  302.2 1.0 copy.12.rank_ref
  303.3 0.0 copy-start.2
  303.3 26.1 %outer.1 = bf16[1024,8192]{1,0:T(8,128)(2,1)} custom-call(f32[1]{0:T(128)S(6)} %div.11.scale_ref, bf16[1024,1024]{1,0:T(8,128)(2,1)} %pad_maximum_fusion.left_ref, s32[1024,1]{1,0:T(8,128)} %copy.12.rank_ref, f32[16,256,512]{2,1,0:T(8,128)} %get-tuple-element.16.weights_ref, f32[16,256,512]{2,1,0:T(8,128)} %get-tuple-element.17.duals_ref), custom_call_target="tpu_custom_call" | custom-call | flops 17179869184 | bytes 33554432 | tf_op jit(solution)/shard_map/outer/pallas_call | solution.py:531
  329.4 0.0 collective-permute-done
  329.4 0.0 copy-done.2
  329.4 1.0 divide_convert_fusion
  (3 shorter events, 0.0 us)
Async XLA Ops:
  206.0 91.4 %copy-start = (bf16[1024,256]{1,0:T(8,128)(2,1)S(1)}, bf16[1024,256]{1,0:T(8,128)(2,1)}, u32[]{:S(2)}) copy-start(bf16[1024,256]{1,0:T(8,128)(2,1)} %param.8) | copy-start | bytes 1572868
  206.0 91.4 %copy-start.1 = (bf16[1024,256]{1,0:T(8,128)(2,1)S(1)}, bf16[1024,256]{1,0:T(8,128)(2,1)}, u32[]{:S(2)}) copy-start(bf16[1024,256]{1,0:T(8,128)(2,1)} %param.7) | copy-start | bytes 1572868
  206.0 93.7 %copy-start.3 = (s32[16384]{0:T(1024)S(1)}, s32[16384]{0:T(1024)}, u32[]{:S(2)}) copy-start(s32[16384]{0:T(1024)} %param.10) | copy-start | bytes 196612
  296.3 33.1 %collective-permute-start = (f32[1024,256]{1,0:T(8,128)}, f32[1024,256]{1,0:T(8,128)S(1)}, u32[]{:S(2)}, u32[]{:S(2)}) collective-permute-start(f32[1024,256]{1,0:T(8,128)} %get-tuple-element.15), channel_id=1, source_target_pairs={{0,1},{1,0},{2,3},{3,2},{4,5},{5,4},{6,7},{7,6},{8,9},{9,8},{10,11... | collective-permute-start | bytes 3145736 | tf_op jit(solution)/shard_map/ppermute | solution.py:526
  303.3 26.1 %copy-start.2 = (f32[1024,256]{1,0:T(8,128)S(1)}, f32[1024,256]{1,0:T(8,128)}, u32[]{:S(2)}) copy-start(f32[1024,256]{1,0:T(8,128)} %get-tuple-element.15) | copy-start | bytes 3145732
